TPU v7x, 128 devices: a whole 4x4x4 slice. The times are simulated.
128 devices in a mesh: dp: 64 (over y, x, z_lo, core), tensor: 2 (over z_hi).
Axes of the slice: x: 4, y: 4, z: 4 (z_hi: 2, z_lo: 2; z = z_hi * 2 + z_lo), core: 2. Of those that a mesh axis runs over, the one named last changes fastest.
Arguments:
- layer_input: bfloat16 [16384, 2048], P(('dp', 'tensor')), may hold values from -6 to 6
- attn_scale: bfloat16 [2048], P('dp'), may hold values from 0.25 to 1.75
- query_weight: bfloat16 [2048, 2048], P('dp', 'tensor'), may hold values from -0.125 to 0.125
- key_weight: bfloat16 [2048, 2048], P('dp', 'tensor'), may hold values from -0.125 to 0.125
- value_weight: bfloat16 [2048, 2048], P('dp', 'tensor'), may hold values from -0.125 to 0.125
- output_weight: bfloat16 [2048, 2048], P('tensor', 'dp'), may hold values from -0.75 to 0.75
- mlp_scale: bfloat16 [2048], P('dp'), may hold values from 0.25 to 1.75
- gate_weight: bfloat16 [2048, 5504], P('dp', 'tensor'), may hold values from -0.125 to 0.125
- up_weight: bfloat16 [2048, 5504], P('dp', 'tensor'), may hold values from -0.125 to 0.125
- down_weight: bfloat16 [5504, 2048], P('tensor', 'dp'), may hold values from -0.078125 to 0.078125
- out_grad: bfloat16 [16384, 2048], P(('dp', 'tensor')), may hold values from -24 to 24
Outputs:
- layer_output: bfloat16 [16384, 2048], P(('dp', 'tensor'))
- input_grad: bfloat16 [16384, 2048], P(('dp', 'tensor'))
- attn_scale_grad: float32 [2048], P('dp')
- query_grad: float32 [2048, 2048], P('dp', 'tensor')
- key_grad: float32 [2048, 2048], P('dp', 'tensor')
- value_grad: float32 [2048, 2048], P('dp', 'tensor')
- output_grad: float32 [2048, 2048], P('tensor', 'dp')
- mlp_scale_grad: float32 [2048], P('dp')
- gate_grad: float32 [2048, 5504], P('dp', 'tensor')
- up_grad: float32 [2048, 5504], P('dp', 'tensor')
- down_grad: float32 [5504, 2048], P('tensor', 'dp')
All inputs are finite; a program needn't handle non-finite values.
Results may differ from a plain program's by a relative error of at most 0.017.
Values may be sent and summed in bfloat16 or wider, within the bound.
No kernel may reach another device: no remote copies, remote signals or barrier semaphores. Data moves between devices by JAX's collectives and lax.ppermute only.
A program may use at most 256 MiB of HBM per device.

v0:
```python
import math

import jax
import jax.numpy as jnp
from jax import lax
from jax.sharding import PartitionSpec as P

HD = 128


epsilon = 1e-05
rope_base = 10000.0
masked_score = -1e30


def plain(left_side, right_side):
    return jnp.dot(left_side, right_side, preferred_element_type=jnp.float32)


def times_t(left_side, right_side):
    return lax.dot_general(
        left_side, right_side, (((1,), (1,)), ((), ())), preferred_element_type=jnp.float32
    )


def left_t(left_side, right_side):
    return lax.dot_general(
        left_side, right_side, (((0,), (0,)), ((), ())), preferred_element_type=jnp.float32
    )


def rms_unit(row_values):
    inv_rms = lax.rsqrt(jnp.mean(row_values * row_values, axis=-1, keepdims=True) + epsilon)
    return (row_values * inv_rms, inv_rms)


def rms_back(grad_normed, unit_rows, inv_rms, gain):
    grad_unit = grad_normed * gain
    inner_mean = jnp.mean(grad_unit * unit_rows, axis=-1, keepdims=True)
    return (
        inv_rms * (grad_unit - unit_rows * inner_mean),
        jnp.sum(grad_normed * unit_rows, axis=0),
    )


def rotary_tables(length, head_size):
    half_size = head_size // 2
    frequency = rope_base ** (-jnp.arange(half_size, dtype=jnp.float32) * 2.0 / head_size)
    angles = jnp.arange(length, dtype=jnp.float32)[:, None] * frequency[None, :]
    return (jnp.cos(angles)[:, None, :], jnp.sin(angles)[:, None, :])


def rotate(values, cosine_table, sine_table, direction):
    half_size = values.shape[-1] // 2
    first_half = values[..., :half_size]
    second_half = values[..., half_size:]
    return jnp.concatenate(
        [
            first_half * cosine_table - direction * (second_half * sine_table),
            second_half * cosine_table + direction * (first_half * sine_table),
        ],
        axis=-1,
    )


def attention_scores(queries, key_rows, factor):
    scores = (
        jnp.einsum("qhd,khd->hqk", queries, key_rows, preferred_element_type=jnp.float32) * factor
    )
    length = queries.shape[0]
    causal = jnp.arange(length)[:, None] >= jnp.arange(length)[None, :]
    return jnp.where(causal[None], scores, masked_score)


def shards(
    layer_input,
    attn_scale,
    query_weight,
    key_weight,
    value_weight,
    output_weight,
    mlp_scale,
    gate_weight,
    up_weight,
    down_weight,
    out_grad,
):
    own_rows = layer_input.shape[0]
    rows_in = lax.all_gather(layer_input, "tensor", axis=0, tiled=True)
    length = rows_in.shape[0]
    full_query, full_key, full_value, full_output, gain_attn = (
        lax.all_gather(query_weight, "dp", axis=0, tiled=True),
        lax.all_gather(key_weight, "dp", axis=0, tiled=True),
        lax.all_gather(value_weight, "dp", axis=0, tiled=True),
        lax.all_gather(output_weight, "dp", axis=1, tiled=True),
        lax.all_gather(attn_scale, "dp", axis=0, tiled=True),
    )
    heads_local = full_query.shape[1] // HD
    factor = 1.0 / math.sqrt(HD)
    cosine_table, sine_table = rotary_tables(length, HD)
    unit_in, rms_in = rms_unit(rows_in.astype(jnp.float32))
    normed_in = (unit_in * gain_attn.astype(jnp.float32)).astype(jnp.bfloat16)
    query_rot = rotate(
        plain(normed_in, full_query).reshape(length, heads_local, HD), cosine_table, sine_table, 1.0
    ).astype(jnp.bfloat16)
    key_rot = rotate(
        plain(normed_in, full_key).reshape(length, heads_local, HD), cosine_table, sine_table, 1.0
    ).astype(jnp.bfloat16)
    value_low = plain(normed_in, full_value).reshape(length, heads_local, HD).astype(jnp.bfloat16)
    scores = attention_scores(query_rot, key_rot, factor)
    row_max = jnp.max(scores, axis=-1, keepdims=True)
    exp_scores = jnp.exp(scores - row_max)
    row_sum = jnp.sum(exp_scores, axis=-1, keepdims=True)
    head_mix = jnp.einsum(
        "hqk,khd->qhd",
        (exp_scores / row_sum).astype(jnp.bfloat16),
        value_low,
        preferred_element_type=jnp.float32,
    )
    heads_cat = head_mix.reshape(length, heads_local * HD).astype(jnp.bfloat16)
    hidden_own = layer_input.astype(jnp.float32) + lax.psum_scatter(
        plain(heads_cat, full_output), "tensor", scatter_dimension=0, tiled=True
    )
    rows_mid = lax.all_gather(hidden_own, "tensor", axis=0, tiled=True)
    full_gate, full_up, full_down, gain_mlp = (
        lax.all_gather(gate_weight, "dp", axis=0, tiled=True),
        lax.all_gather(up_weight, "dp", axis=0, tiled=True),
        lax.all_gather(down_weight, "dp", axis=1, tiled=True),
        lax.all_gather(mlp_scale, "dp", axis=0, tiled=True),
    )
    unit_mid, rms_mid = rms_unit(rows_mid)
    normed_mid = (unit_mid * gain_mlp.astype(jnp.float32)).astype(jnp.bfloat16)
    gate_pre = plain(normed_mid, full_gate)
    up_pre = plain(normed_mid, full_up)
    sigmoid_gate = jax.nn.sigmoid(gate_pre)
    swish_gate = gate_pre * sigmoid_gate
    activation = (swish_gate * up_pre).astype(jnp.bfloat16)
    layer_output = (
        hidden_own
        + lax.psum_scatter(
            plain(activation, full_down).astype(jnp.bfloat16),
            "tensor",
            scatter_dimension=0,
            tiled=True,
        ).astype(jnp.float32)
    ).astype(jnp.bfloat16)
    grad_rows = lax.all_gather(out_grad, "tensor", axis=0, tiled=True)
    full_gate, full_up, full_down, gain_mlp = (
        lax.all_gather(gate_weight, "dp", axis=0, tiled=True),
        lax.all_gather(up_weight, "dp", axis=0, tiled=True),
        lax.all_gather(down_weight, "dp", axis=1, tiled=True),
        lax.all_gather(mlp_scale, "dp", axis=0, tiled=True),
    )
    grad_act = times_t(grad_rows, full_down)
    down_full = left_t(activation, grad_rows)
    grad_gate = (
        grad_act * up_pre * (sigmoid_gate + gate_pre * sigmoid_gate * (1.0 - sigmoid_gate))
    ).astype(jnp.bfloat16)
    grad_up = (grad_act * swish_gate).astype(jnp.bfloat16)
    gate_full = left_t(normed_mid, grad_gate)
    up_full = left_t(normed_mid, grad_up)
    grad_mid = lax.psum(
        (times_t(grad_gate, full_gate) + times_t(grad_up, full_up)).astype(jnp.bfloat16), "tensor"
    ).astype(jnp.float32)
    grad_norm_mid, mlp_gain_full = rms_back(
        grad_mid, unit_mid, rms_mid, gain_mlp.astype(jnp.float32)
    )
    grad_hidden = grad_rows.astype(jnp.float32) + grad_norm_mid
    gate_part, up_part, down_part, mlp_gain_part = (
        lax.psum_scatter(gate_full, "dp", scatter_dimension=0, tiled=True),
        lax.psum_scatter(up_full, "dp", scatter_dimension=0, tiled=True),
        lax.psum_scatter(down_full, "dp", scatter_dimension=1, tiled=True),
        lax.psum_scatter(mlp_gain_full, "dp", scatter_dimension=0, tiled=True),
    )
    full_query, full_key, full_value, full_output, gain_attn = (
        lax.all_gather(query_weight, "dp", axis=0, tiled=True),
        lax.all_gather(key_weight, "dp", axis=0, tiled=True),
        lax.all_gather(value_weight, "dp", axis=0, tiled=True),
        lax.all_gather(output_weight, "dp", axis=1, tiled=True),
        lax.all_gather(attn_scale, "dp", axis=0, tiled=True),
    )
    hidden_low = grad_hidden.astype(jnp.bfloat16)
    output_full = left_t(heads_cat, hidden_low)
    grad_heads = (
        times_t(hidden_low, full_output).reshape(length, heads_local, HD).astype(jnp.bfloat16)
    )
    scores = attention_scores(query_rot, key_rot, factor)
    soft_weights = jnp.exp(scores - row_max) / row_sum
    grad_soft = jnp.einsum(
        "qhd,khd->hqk", grad_heads, value_low, preferred_element_type=jnp.float32
    )
    grad_values = (
        jnp.einsum(
            "hqk,qhd->khd",
            soft_weights.astype(jnp.bfloat16),
            grad_heads,
            preferred_element_type=jnp.float32,
        )
        .reshape(length, heads_local * HD)
        .astype(jnp.bfloat16)
    )
    row_inner = jnp.sum(grad_soft * soft_weights, axis=-1, keepdims=True)
    grad_scores = (soft_weights * (grad_soft - row_inner)).astype(jnp.bfloat16)
    grad_queries = (
        rotate(
            jnp.einsum("hqk,khd->qhd", grad_scores, key_rot, preferred_element_type=jnp.float32)
            * factor,
            cosine_table,
            sine_table,
            -1.0,
        )
        .reshape(length, heads_local * HD)
        .astype(jnp.bfloat16)
    )
    grad_keys = (
        rotate(
            jnp.einsum("hqk,qhd->khd", grad_scores, query_rot, preferred_element_type=jnp.float32)
            * factor,
            cosine_table,
            sine_table,
            -1.0,
        )
        .reshape(length, heads_local * HD)
        .astype(jnp.bfloat16)
    )
    query_full = left_t(normed_in, grad_queries)
    key_full = left_t(normed_in, grad_keys)
    value_full = left_t(normed_in, grad_values)
    grad_in = lax.psum(
        (
            times_t(grad_queries, full_query)
            + times_t(grad_keys, full_key)
            + times_t(grad_values, full_value)
        ).astype(jnp.bfloat16),
        "tensor",
    ).astype(jnp.float32)
    grad_norm_in, attn_gain_full = rms_back(grad_in, unit_in, rms_in, gain_attn.astype(jnp.float32))
    input_full = grad_hidden + grad_norm_in
    row_start = lax.axis_index("tensor") * own_rows
    input_grad = lax.dynamic_slice_in_dim(input_full, row_start, own_rows, 0).astype(jnp.bfloat16)
    query_part, key_part, value_part, output_part, attn_gain_part = (
        lax.psum_scatter(query_full, "dp", scatter_dimension=0, tiled=True),
        lax.psum_scatter(key_full, "dp", scatter_dimension=0, tiled=True),
        lax.psum_scatter(value_full, "dp", scatter_dimension=0, tiled=True),
        lax.psum_scatter(output_full, "dp", scatter_dimension=1, tiled=True),
        lax.psum_scatter(attn_gain_full, "dp", scatter_dimension=0, tiled=True),
    )
    return (
        layer_output,
        input_grad,
        attn_gain_part,
        query_part,
        key_part,
        value_part,
        output_part,
        mlp_gain_part,
        gate_part,
        up_part,
        down_part,
    )


def solution(mesh):
    return jax.shard_map(
        shards,
        mesh=mesh,
        in_specs=(
            P(("dp", "tensor"), None),
            P("dp"),
            P("dp", "tensor"),
            P("dp", "tensor"),
            P("dp", "tensor"),
            P("tensor", "dp"),
            P("dp"),
            P("dp", "tensor"),
            P("dp", "tensor"),
            P("tensor", "dp"),
            P(("dp", "tensor"), None),
        ),
        out_specs=(
            P(("dp", "tensor"), None),
            P(("dp", "tensor"), None),
            P("dp"),
            P("dp", "tensor"),
            P("dp", "tensor"),
            P("dp", "tensor"),
            P("tensor", "dp"),
            P("dp"),
            P("dp", "tensor"),
            P("dp", "tensor"),
            P("tensor", "dp"),
        ),
        check_vma=False,
    )
```

profile of v0, /device:TPU:0, one launch (start us, length us, event | category | flops | bytes accessed | tf_op | source)
XLA Modules:
  0.0 3258.1 jit_solution(4708363947633434157)
XLA Ops:
  14.3 147.1 %all-reduce.5 = (bf16[2048]{0:T(1024)(128)(2,1)S(1)}, bf16[2048]{0:T(1024)(128)(2,1)S(1)}) all-reduce(bf16[2048]{0:T(1024)(128)(2,1)S(1)} %dynamic-update-slice, bf16[2048]{0:T(1024)(128)(2,1)S(1)} %dynamic-update-slice.1), channel_id=1, replica_groups=mesh['dp'=64,'tensor'=2] {'dp'}, use_global_device_ids=true, to_apply=%add | all-reduce | flops 4096 | bytes 16384
  163.6 3.9 convolution_bitcast_fusion.1
  167.7 84.2 %all-gather.17.cloned.1.call-done = bf16[2048,1024]{1,0:T(8,128)(2,1)} async-done(((bf16[32,1024]{1,0:T(8,128)(2,1)}), bf16[2048,1024]{1,0:T(8,128)(2,1)}) %all-gather.17.cloned.1.call-update) | async-done | bytes 4194320 | tf_op jit(solution)/shard_map/all_gather | solution.py:93
  252.0 3.5 convolution_bitcast_fusion
  256.3 2.1 subtract_convert_fusion.3
  258.4 2.7 fusion.43
  261.1 97.3 %all-gather.13.cloned.1.call-done = bf16[2048,1024]{1,0:T(8,128)(2,1)} async-done(((bf16[32,1024]{1,0:T(8,128)(2,1)}), bf16[2048,1024]{1,0:T(8,128)(2,1)}) %all-gather.13.cloned.1.call-update) | async-done | bytes 4194320 | tf_op jit(solution)/shard_map/all_gather | solution.py:94
  358.4 3.5 fusion.15
  363.9 101.0 %all-gather.19.cloned.1.call-done = bf16[1024,2048]{0,1:T(8,128)(2,1)} async-done(((bf16[1024,32]{0,1:T(8,128)(2,1)}), bf16[1024,2048]{0,1:T(8,128)(2,1)}) %all-gather.19.cloned.1.call-update) | async-done | bytes 4194320 | tf_op jit(solution)/shard_map/all_gather | solution.py:95
  465.0 5.0 fusion.44
  470.0 35.1 %reduce-scatter.10.cloned.1.call-done = f32[128,2048]{1,0:T(8,128)} async-done(((f32[256,2048]{1,0:T(8,128)}), f32[128,2048]{1,0:T(8,128)}) %reduce-scatter.10.cloned.1.call-update) | async-done | bytes 1048592 | tf_op jit(solution)/shard_map/reduce_scatter | solution.py:121
  505.2 2.3 convert_add_fusion
  510.6 33.6 %all-gather.21.cloned.1.call-done = f32[256,2048]{1,0:T(8,128)} async-done(((f32[128,2048]{1,0:T(8,128)}), f32[256,2048]{1,0:T(8,128)}) %all-gather.21.cloned.1.call-update) | async-done | bytes 2097168 | tf_op jit(solution)/shard_map/all_gather | solution.py:124
  544.1 2.0 multiply_reduce_fusion.2
  547.6 114.2 %all-gather.23.cloned.1.call-done = bf16[2048,2752]{1,0:T(8,128)(2,1)} async-done(((bf16[32,2752]{1,0:T(8,128)(2,1)}), bf16[2048,2752]{1,0:T(8,128)(2,1)}) %all-gather.23.cloned.1.call-update) | async-done | bytes 11272208 | tf_op jit(solution)/shard_map/all_gather | solution.py:126
  661.8 10.8 fusion.45
  672.6 107.0 %all-gather.25.cloned.1.call-done = bf16[2048,2752]{1,0:T(8,128)(2,1)} async-done(((bf16[32,2752]{1,0:T(8,128)(2,1)}), bf16[2048,2752]{1,0:T(8,128)(2,1)}) %all-gather.25.cloned.1.call-update) | async-done | bytes 11272208 | tf_op jit(solution)/shard_map/all_gather | solution.py:127
  779.6 10.7 fusion.46
  790.3 15.7 all-gather.29.cloned.1.call-done
  806.0 117.7 %all-gather.27.cloned.1.call-done = bf16[2752,2048]{0,1:T(8,128)(2,1)} async-done(((bf16[2752,32]{0,1:T(8,128)(2,1)}), bf16[2752,2048]{0,1:T(8,128)(2,1)}) %all-gather.27.cloned.1.call-update) | async-done | bytes 11272208 | tf_op jit(solution)/shard_map/all_gather | solution.py:128
  923.7 13.0 multiply_convert_fusion
  936.8 7.1 fusion.47
  943.9 8.5 fusion.1
  952.5 8.9 convolution_convert_fusion
  961.6 38.5 %all-reduce.9.cloned.1.call-done = bf16[256,2048]{1,0:T(8,128)(2,1)} async-done(((bf16[256,2048]{1,0:T(8,128)(2,1)}), bf16[256,2048]{1,0:T(8,128)(2,1)}) %all-reduce.9.cloned.1.call-update) | async-done | bytes 1048592 | tf_op jit(solution)/shard_map/psum | solution.py:162
  1000.1 2.1 fusion.9
  1005.2 2.1 convolution_convert_fusion.3
  1007.3 2.1 copy.86
  1009.4 1.8 multiply_reduce_fusion.1
  1016.2 2.4 convolution_convert_fusion.1
  1023.6 2.3 fusion.2
  1026.2 4.7 fusion.39
  1031.0 4.8 fusion.38
  1035.9 4.7 fusion.37
  1042.2 5.7 fusion.24
  1048.0 12.8 fusion.49
  1061.0 12.7 fusion.50
  1073.8 12.5 fusion.51
  1087.1 2.3 add_convert_fusion.2
  1089.3 3.9 fusion.10
  1093.3 280.0 %all-reduce.4 = (f32[2048]{0:T(1024)S(1)}, f32[2048]{0:T(1024)S(1)}) all-reduce(f32[2048]{0:T(1024)S(1)} %get-tuple-element.13, f32[2048]{0:T(1024)S(1)} %get-tuple-element.11), channel_id=4, replica_groups=mesh['dp'=64,'tensor'=2] {'dp'}, use_global_device_ids=true, to_apply=%region_12.13.clone | all-reduce | flops 4096 | bytes 32768
  1374.5 2.6 fusion.16
  1377.5 298.2 %reduce-scatter.16.cloned.1.call-done = f32[32,1024]{1,0:T(8,128)} async-done(((f32[2048,1024]{1,0:T(8,128)}), f32[32,1024]{1,0:T(8,128)}) %reduce-scatter.16.cloned.1.call-update) | async-done | bytes 131088 | tf_op jit(solution)/shard_map/reduce_scatter | solution.py:243
  1675.7 298.7 %reduce-scatter.18.cloned.1.call-done = f32[32,1024]{1,0:T(8,128)} async-done(((f32[2048,1024]{1,0:T(8,128)}), f32[32,1024]{1,0:T(8,128)}) %reduce-scatter.18.cloned.1.call-update) | async-done | bytes 131088 | tf_op jit(solution)/shard_map/reduce_scatter | solution.py:244
  1974.4 298.4 %reduce-scatter.20.cloned.1.call-done = f32[1024,32]{0,1:T(8,128)} async-done(((f32[1024,2048]{0,1:T(8,128)}), f32[1024,32]{0,1:T(8,128)}) %reduce-scatter.20.cloned.1.call-update) | async-done | bytes 131088 | tf_op jit(solution)/shard_map/reduce_scatter | solution.py:245
  2272.8 325.3 %reduce-scatter.22.cloned.1.call-done = f32[32,2752]{1,0:T(8,128)} async-done(((f32[2048,2752]{1,0:T(8,128)}), f32[32,2752]{1,0:T(8,128)}) %reduce-scatter.22.cloned.1.call-update) | async-done | bytes 352272 | tf_op jit(solution)/shard_map/reduce_scatter | solution.py:170
  2598.2 325.4 %reduce-scatter.24.cloned.1.call-done = f32[32,2752]{1,0:T(8,128)} async-done(((f32[2048,2752]{1,0:T(8,128)}), f32[32,2752]{1,0:T(8,128)}) %reduce-scatter.24.cloned.1.call-update) | async-done | bytes 352272 | tf_op jit(solution)/shard_map/reduce_scatter | solution.py:171
  2923.6 327.3 %reduce-scatter.26.cloned.1.call-done = f32[2752,32]{0,1:T(8,128)} async-done(((f32[2752,2048]{0,1:T(8,128)}), f32[2752,32]{0,1:T(8,128)}) %reduce-scatter.26.cloned.1.call-update) | async-done | bytes 352272 | tf_op jit(solution)/shard_map/reduce_scatter | solution.py:172
  (122 shorter events, 33.4 us)
Async XLA Ops:
  7.2 154.9 %all-gather.11.cloned.1.call-start = ((), (), s32[]{:S(2)}) async-start(), calls=%async_computation.9 | async-start | bytes 1572864 | tf_op jit(solution)/shard_map/all_gather | solution.py:89
  7.9 155.7 %all-gather.15.cloned.1.call-start = ((), (), s32[]{:S(2)}) async-start(), calls=%async_computation.11 | async-start | bytes 4259840 | tf_op jit(solution)/shard_map/all_gather | solution.py:92
  8.7 243.3 %all-gather.17.cloned.1.call-start = ((), (), s32[]{:S(2)}) async-start(), calls=%async_computation.12 | async-start | bytes 4259840 | tf_op jit(solution)/shard_map/all_gather | solution.py:93
  9.4 349.1 %all-gather.13.cloned.1.call-start = ((), (), s32[]{:S(2)}) async-start(), calls=%async_computation.10 | async-start | bytes 4259840 | tf_op jit(solution)/shard_map/all_gather | solution.py:94
  10.0 455.0 %all-gather.19.cloned.1.call-start = ((), (), s32[]{:S(2)}) async-start(), calls=%async_computation.13 | async-start | bytes 4259840 | tf_op jit(solution)/shard_map/all_gather | solution.py:95
  10.6 494.6 %reduce-scatter.10.cloned.1.call-start = ((), (), s32[]{:S(2)}) async-start(), calls=%async_computation.14 | async-start | bytes 3145728 | tf_op jit(solution)/shard_map/reduce_scatter | solution.py:121
  163.6 88.4 %copy-start = (bf16[256,2048]{1,0:T(8,128)(2,1)S(1)}, bf16[256,2048]{1,0:T(8,128)(2,1)}, u32[]{:S(2)}) copy-start(bf16[256,2048]{1,0:T(8,128)(2,1)} %all-gather.11.cloned.1.call-done) | copy-start | bytes 3145732
  261.1 100.8 %copy-start.8 = (f32[8,256,256]{1,2,0:T(8,128)}, f32[8,256,256]{1,2,0:T(8,128)S(1)}, u32[]{:S(2)}) copy-start(f32[8,256,256]{1,2,0:T(8,128)S(1)} %get-tuple-element.45) | copy-start | bytes 6291460
  361.9 0.8 copy-start.19
  469.9 35.2 %copy-start.7 = (bf16[128,2048]{1,0:T(8,128)(2,1)S(1)}, bf16[128,2048]{1,0:T(8,128)(2,1)}, u32[]{:S(2)}) copy-start(bf16[128,2048]{1,0:T(8,128)(2,1)} %param.11) | copy-start | bytes 1572868
  470.0 74.2 %all-gather.21.cloned.1.call-start = ((), (), s32[]{:S(2)}) async-start(), calls=%async_computation.15 | async-start | bytes 3145728 | tf_op jit(solution)/shard_map/all_gather | solution.py:124
  507.5 154.3 %all-gather.23.cloned.1.call-start = ((), (), s32[]{:S(2)}) async-start(), calls=%async_computation.16 | async-start | bytes 11714560 | tf_op jit(solution)/shard_map/all_gather | solution.py:126
  508.2 271.3 %all-gather.25.cloned.1.call-start = ((), (), s32[]{:S(2)}) async-start(), calls=%async_computation.17 | async-start | bytes 11714560 | tf_op jit(solution)/shard_map/all_gather | solution.py:127
  509.0 297.1 %all-gather.29.cloned.1.call-start = ((), (), s32[]{:S(2)}) async-start(), calls=%async_computation.20 | async-start | bytes 1572864 | tf_op jit(solution)/shard_map/all_gather | solution.py:147
  509.6 414.1 %all-gather.27.cloned.1.call-start = ((), (), s32[]{:S(2)}) async-start(), calls=%async_computation.18 | async-start | bytes 11714560 | tf_op jit(solution)/shard_map/all_gather | solution.py:128
  510.3 489.8 %all-reduce.9.cloned.1.call-start = ((), (), s32[]{:S(2)}) async-start(), calls=%async_computation.21 | async-start | bytes 2097152 | tf_op jit(solution)/shard_map/psum | solution.py:162
  544.1 2.2 copy-start.1
  936.7 7.1 copy-start.15
  936.7 7.1 copy-start.14
  952.4 134.6 %reduce-scatter.12.cloned.1.call-start = ((), (), s32[]{:S(2)}) async-start(), calls=%async_computation.19 | async-start | bytes 1572864 | tf_op jit(solution)/shard_map/reduce_scatter | solution.py:140
  961.4 127.9 %all-reduce.11.cloned.1.call-start = ((), (), s32[]{:S(2)}) async-start(), calls=%async_computation.22 | async-start | bytes 2097152 | tf_op jit(solution)/shard_map/psum | solution.py:229
  1000.1 2.2 copy-start.5
  1000.1 2.2 copy-start.6
  1002.3 2.9 copy-start.18
  1002.9 1.3 copy-start.2
  1005.2 4.2 copy-start.9
  1011.2 1.0 copy-start.12
  1011.2 1.2 copy-start.13
  1012.4 1.0 copy-start.10
  1012.4 1.2 copy-start.11
  1016.2 3.0 copy-start.16
  1019.2 2.2 copy-start.4
  1021.4 2.2 copy-start.17
  1026.0 351.5 %reduce-scatter.14.cloned.1.call-start = ((), (), s32[]{:S(2)}) async-start(), calls=%async_computation.23 | async-start | bytes 8519680 | tf_op jit(solution)/shard_map/reduce_scatter | solution.py:242
  1031.0 644.8 %reduce-scatter.16.cloned.1.call-start = ((), (), s32[]{:S(2)}) async-start(), calls=%async_computation.24 | async-start | bytes 8519680 | tf_op jit(solution)/shard_map/reduce_scatter | solution.py:243
  1035.8 938.6 %reduce-scatter.18.cloned.1.call-start = ((), (), s32[]{:S(2)}) async-start(), calls=%async_computation.25 | async-start | bytes 8519680 | tf_op jit(solution)/shard_map/reduce_scatter | solution.py:244
  1040.6 1.6 copy-start.3
  1040.6 1232.2 %reduce-scatter.20.cloned.1.call-start = ((), (), s32[]{:S(2)}) async-start(), calls=%async_computation.26 | async-start | bytes 8519680 | tf_op jit(solution)/shard_map/reduce_scatter | solution.py:245
  1047.9 1550.3 %reduce-scatter.22.cloned.1.call-start = ((), (), s32[]{:S(2)}) async-start(), calls=%async_computation.27 | async-start | bytes 23429120 | tf_op jit(solution)/shard_map/reduce_scatter | solution.py:170
  1060.7 1862.8 %reduce-scatter.24.cloned.1.call-start = ((), (), s32[]{:S(2)}) async-start(), calls=%async_computation.28 | async-start | bytes 23429120 | tf_op jit(solution)/shard_map/reduce_scatter | solution.py:171
  1073.7 2177.1 %reduce-scatter.26.cloned.1.call-start = ((), (), s32[]{:S(2)}) async-start(), calls=%async_computation.29 | async-start | bytes 23429120 | tf_op jit(solution)/shard_map/reduce_scatter | solution.py:172
Sparse Core Ops, SparseCore 0:
  9.7 28.5 all-gather.10
  40.0 105.0 all-gather.14
  146.8 105.0 all-gather.16
  253.5 104.8 all-gather.12
  360.0 104.9 all-gather.18
  470.1 35.0 reduce-scatter.9
  507.6 36.4 all-gather.20
  546.0 115.7 all-gather.22
  663.6 115.9 all-gather.24
  781.2 24.8 all-gather.28
  807.9 115.7 all-gather.26
  952.6 47.4 all-reduce.8
  1002.4 23.6 reduce-scatter.11
  1028.6 47.3 all-reduce.10
  1078.8 298.6 reduce-scatter.13
  1380.3 295.3 reduce-scatter.15
  1678.5 295.8 reduce-scatter.17
  1977.2 295.5 reduce-scatter.19
  2275.8 322.2 reduce-scatter.21
  2601.0 322.5 reduce-scatter.23
  2926.6 324.2 reduce-scatter.25
where the time goes:
time: 3270 us; the launch traced here: 3260 us
  waiting for transfers between devices  2620 us (80%)
  blocking collectives  427 us (13%)
  matrix products  149 us (5%)
    unnamed x2, blocking collectives  427 us
    reduce_scatter x1, waiting for transfers between devices, shards(): lax.psum_scatter(down_full, 'dp', scatter_dimension=1, tiled=True)  327 us
    reduce_scatter x1, waiting for transfers between devices, shards(): lax.psum_scatter(up_full, 'dp', scatter_dimension=0, tiled=True)  325 us
    reduce_scatter x1, waiting for transfers between devices, shards(): lax.psum_scatter(gate_full, 'dp', scatter_dimension=0, tiled=True)  325 us
    reduce_scatter x1, waiting for transfers between devices, shards(): lax.psum_scatter(value_full, 'dp', scatter_dimension=0, tiled=True)  299 us
    reduce_scatter x1, waiting for transfers between devices, shards(): lax.psum_scatter(output_full, 'dp', scatter_dimension=1, tiled=True)  298 us
    reduce_scatter x1, waiting for transfers between devices, shards(): lax.psum_scatter(key_full, 'dp', scatter_dimension=0, tiled=True)  298 us
    all_gather x1, waiting for transfers between devices, shards(): lax.all_gather(down_weight, 'dp', axis=1, tiled=True)  118 us
  transfers between devices with their start and end apart: 21, of which 17 were waited for; matrix products, arithmetic and copies ran while one was open for 4% of the time, Pallas kernels for 0%

commit v1 on v0

v1 whole, which is shorter than its diff:
```python
import math

import jax
import jax.numpy as jnp
from jax import lax
from jax.sharding import Mesh, PartitionSpec as P

HD = 128
EPSILON = 1e-05
ROPE_BASE = 10000.0
MASKED = -1e30
BF = jnp.bfloat16
F32 = jnp.float32

GROUP = ("y", "x", "l", "c")
RING = ("l", "t")
PLACES = (0, 2, 1, 3)


def plain(left, right):
    return jnp.dot(left, right, preferred_element_type=F32)


def times_t(left, right):
    return lax.dot_general(left, right, (((1,), (1,)), ((), ())), preferred_element_type=F32)


def left_t(left, right):
    return lax.dot_general(left, right, (((0,), (0,)), ((), ())), preferred_element_type=F32)


def move(values, axis, distance):
    place = PLACES if axis == RING else range(4)
    return lax.ppermute(values, axis, [(place[s], place[(s + distance) % 4]) for s in range(4)])


def swap(values, axis):
    return lax.ppermute(values, axis, [(0, 1), (1, 0)])


def gather_rows(own):
    back1 = move(own, RING, -1)
    back3 = move(own, RING, 1)
    back2 = move(own, RING, 2)
    mine = [own, back2, back1, back3]
    return jnp.concatenate(mine + [swap(block, "c") for block in mine], axis=0)


def scatter_rows(partial):
    rows = partial.shape[0] // 8
    other = swap(partial[4 * rows :], "c")
    blocks = partial[: 4 * rows].astype(F32) + other.astype(F32)
    to2, to1, to3 = (blocks[rows * i : rows * (i + 1)].astype(BF) for i in (1, 2, 3))
    got1 = move(to1, RING, 1)
    got3 = move(to3, RING, -1)
    got2 = move(to2, RING, 2)
    return blocks[:rows] + got1.astype(F32) + got3.astype(F32) + got2.astype(F32)


def exchange(pieces):
    core, low = lax.axis_index("c"), lax.axis_index("l")
    mine = jnp.where(core == 0, pieces[:, 0], pieces[:, 1])
    theirs = swap(jnp.where(core == 0, pieces[:, 1], pieces[:, 0]), "c")
    cores = jnp.stack(
        [jnp.where(core == 0, mine, theirs), jnp.where(core == 0, theirs, mine)], axis=1
    )
    mine = jnp.where(low == 0, cores[0], cores[1])
    theirs = swap(jnp.where(low == 0, cores[1], cores[0]), "l")
    return jnp.stack([jnp.where(low == 0, mine, theirs), jnp.where(low == 0, theirs, mine)], axis=0)


def split_pieces(weight, width):
    rows, columns = weight.shape
    pieces = weight.reshape(rows, 4, columns // 4)
    return jnp.pad(pieces, ((0, 0), (0, 0), (0, width - columns // 4)))


def to_pieces(weights, widths):
    joined = jnp.concatenate([split_pieces(w, n) for w, n in zip(weights, widths)], axis=2)
    rows = joined.shape[0]
    return joined.transpose(1, 0, 2).reshape(2, 2, rows, joined.shape[2])


def gather_line(block, axis):
    index = lax.axis_index(axis)
    found = jnp.zeros((4,) + block.shape, block.dtype)
    for distance, values in (
        (0, block),
        (1, move(block, axis, -1)),
        (3, move(block, axis, 1)),
        (2, move(block, axis, 2)),
    ):
        found = lax.dynamic_update_index_in_dim(found, values, (index + distance) % 4, 0)
    return found


def gather_plane(block, first):
    second = "x" if first == "y" else "y"
    index = lax.axis_index(second)
    line = gather_line(block, first)
    place = 0 if second == "y" else 1
    found = jnp.zeros((4, 4) + block.shape, block.dtype)
    for distance, values in (
        (0, line),
        (1, move(line, second, -1)),
        (3, move(line, second, 1)),
        (2, move(line, second, 2)),
    ):
        found = lax.dynamic_update_index_in_dim(found, values, (index + distance) % 4, place)
    return found.reshape(16 * block.shape[0], block.shape[1])


def reduce_line(blocks, axis, place):
    index = lax.axis_index(axis)

    def part(distance):
        return lax.dynamic_index_in_dim(blocks, (index + distance) % 4, place, keepdims=False)

    total = part(0).astype(F32)
    for distance in (1, 3, 2):
        total = total + move(part(distance), axis, distance).astype(F32)
    return total


def reduce_plane(partial, first):
    rows, columns = partial.shape
    blocks = partial.reshape(4, 4, rows // 16, columns)
    second = "x" if first == "y" else "y"
    line = reduce_line(blocks, first, 0 if first == "y" else 1).astype(BF)
    return reduce_line(line, second, 0)


def rms_unit(rows):
    inv = lax.rsqrt(jnp.mean(rows * rows, axis=-1, keepdims=True) + EPSILON)
    return rows * inv, inv


def rms_back(grad_unit, unit, inv):
    return inv * (grad_unit - unit * jnp.mean(grad_unit * unit, axis=-1, keepdims=True))


def positions(half):
    ring = lax.axis_index("t") * 2 + lax.axis_index("l")
    rows = jnp.arange(2 * half, dtype=jnp.int32)
    starts = jnp.stack([ring // 2, ((ring + 1) % 4) // 2]) * half
    return (rows[None, :] + starts[:, None]) % (2 * half)


def rotary_tables(place):
    half_size = HD // 2
    frequency = ROPE_BASE ** (-jnp.arange(half_size, dtype=F32) * 2.0 / HD)
    length = place.shape[-1]
    angles = jnp.arange(length, dtype=F32)[:, None] * frequency[None, :]
    tables = []
    for table in (jnp.cos(angles), jnp.sin(angles)):
        turned = jnp.roll(table, length // 2, axis=0)
        both = jnp.stack([jnp.where(place[i, 0] == 0, table, turned) for i in range(2)])
        tables.append(jnp.concatenate([both, both], axis=0))
    return tables


def rotate(values, cosine, sine):
    half_size = HD // 2
    first, second = values[..., :half_size], values[..., half_size:]
    return jnp.concatenate([first * cosine - second * sine, second * cosine + first * sine], -1)


def batched(left, right, left_dim, right_dim):
    return lax.dot_general(
        left, right, (((left_dim,), (right_dim,)), ((0,), (0,))), preferred_element_type=F32
    )


def shards(
    layer_input,
    attn_scale,
    query_weight,
    key_weight,
    value_weight,
    output_weight,
    mlp_scale,
    gate_weight,
    up_weight,
    down_weight,
    out_grad,
):
    half, width = layer_input.shape
    length = 2 * half
    tokens = 8 * half
    gain_attn = attn_scale.astype(F32)[:, None]
    gain_mlp = mlp_scale.astype(F32)[:, None]
    part = query_weight.shape[1] // 4
    heads = part // HD
    units = gate_weight.shape[1] // 4
    wide = -(-units // 128) * 128
    factor = 1.0 / math.sqrt(HD)

    def scaled(weight, gain):
        return (weight.astype(F32) * gain).astype(BF)

    attn_pieces = to_pieces(
        [
            scaled(query_weight, gain_attn),
            scaled(key_weight, gain_attn),
            scaled(value_weight, gain_attn),
            output_weight.T,
        ],
        [part] * 4,
    )
    mlp_pieces = to_pieces(
        [scaled(gate_weight, gain_mlp), scaled(up_weight, gain_mlp), down_weight.T], [wide] * 3
    )
    attn_block = exchange(attn_pieces).reshape(-1, 4 * part)
    qk_weight = gather_plane(attn_block[:, : 2 * part], "x")
    vo_weight = gather_plane(attn_block[:, 2 * part :], "y")
    mlp_block = exchange(mlp_pieces).reshape(-1, 3 * wide)
    mlp_weight = lax.all_gather(mlp_block, ("y", "x"), axis=0, tiled=True)
    gu_weight, down_t = mlp_weight[:, : 2 * wide], mlp_weight[:, 2 * wide :]

    unit_in, inv_in = rms_unit(layer_input.astype(F32))
    rows_in = gather_rows(unit_in.astype(BF))
    place = positions(half)
    cosine, sine = rotary_tables(place)
    causal = place[:, :, None] >= place[:, None, :]
    causal = jnp.concatenate([causal, causal], axis=0)
    qk = plain(rows_in, qk_weight)
    value_all = plain(rows_in, vo_weight[:, :part]).astype(BF).reshape(4, length, part)
    output_t = vo_weight[:, part:]

    def head(values, index):
        return values[:, index * HD : (index + 1) * HD].reshape(4, length, HD)

    kept, mixes = [], []
    for i in range(heads):
        query = rotate(head(qk[:, :part], i), cosine, sine).astype(BF)
        key = rotate(head(qk[:, part:], i), cosine, sine).astype(BF)
        value = value_all[:, :, i * HD : (i + 1) * HD]
        scores = jnp.where(causal, batched(query, key, 2, 2) * factor, MASKED)
        weights = jnp.exp(scores - jnp.max(scores, axis=-1, keepdims=True))
        soft = weights / jnp.sum(weights, axis=-1, keepdims=True)
        mixes.append(batched(soft.astype(BF), value, 2, 1).astype(BF))
        kept.append((query, key, value, soft))
    heads_cat = jnp.concatenate(mixes, axis=-1).reshape(tokens, part)
    hidden = layer_input.astype(F32) + scatter_rows(times_t(heads_cat, output_t).astype(BF))

    unit_mid, inv_mid = rms_unit(hidden)
    rows_mid = gather_rows(unit_mid.astype(BF))
    gate_up = plain(rows_mid, gu_weight)
    gate, up = gate_up[:, :wide], gate_up[:, wide:]
    sigmoid = jax.nn.sigmoid(gate)
    swish = gate * sigmoid
    activation = (swish * up).astype(BF)
    layer_output = (hidden + scatter_rows(times_t(activation, down_t).astype(BF))).astype(BF)

    rows_grad = gather_rows(out_grad)
    grad_act = plain(rows_grad, down_t)
    grad_gate = (grad_act * up * (sigmoid + swish * (1.0 - sigmoid))).astype(BF)
    grad_up = (grad_act * swish).astype(BF)
    grad_gu = jnp.concatenate([grad_gate, grad_up], axis=1)
    grad_unit_mid = scatter_rows(times_t(grad_gu, gu_weight).astype(BF))
    mlp_partial = jnp.concatenate([left_t(rows_mid, grad_gu), left_t(rows_grad, activation)], axis=1)
    mlp_sum = lax.psum_scatter(
        mlp_partial.astype(BF), ("y", "x"), scatter_dimension=0, tiled=True
    )
    grad_hidden = out_grad.astype(F32) + rms_back(grad_unit_mid, unit_mid, inv_mid)

    rows_hidden = gather_rows(grad_hidden.astype(BF))
    grad_heads = plain(rows_hidden, output_t).astype(BF)
    output_partial = left_t(rows_hidden, heads_cat)
    grad_q, grad_k, grad_v = [], [], []
    for i in range(heads):
        query, key, value, soft = kept[i]
        grad_mix = head(grad_heads, i)
        grad_soft = batched(grad_mix, value, 2, 2)
        grad_v.append(batched(soft.astype(BF), grad_mix, 1, 1).astype(BF))
        inner = jnp.sum(grad_soft * soft, axis=-1, keepdims=True)
        grad_scores = (soft * (grad_soft - inner)).astype(BF)
        back_q = batched(grad_scores, key, 2, 1) * factor
        back_k = batched(grad_scores, query, 1, 1) * factor
        grad_q.append(rotate(back_q, cosine, -sine).astype(BF))
        grad_k.append(rotate(back_k, cosine, -sine).astype(BF))
    grad_qk = jnp.concatenate(grad_q + grad_k, axis=-1).reshape(tokens, 2 * part)
    grad_value = jnp.concatenate(grad_v, axis=-1).reshape(tokens, part)
    qk_sum = reduce_plane(left_t(rows_in, grad_qk).astype(BF), "x")
    vo_partial = jnp.concatenate([left_t(rows_in, grad_value), output_partial], axis=1)
    vo_sum = reduce_plane(vo_partial.astype(BF), "y")
    grad_unit_in = scatter_rows(
        (times_t(grad_qk, qk_weight) + times_t(grad_value, vo_weight[:, :part])).astype(BF)
    )
    input_grad = (grad_hidden + rms_back(grad_unit_in, unit_in, inv_in)).astype(BF)

    def owned(total):
        return exchange(total.astype(BF).reshape(2, 2, -1, total.shape[1]))

    def whole(pieces, start, size):
        piece = pieces[..., start : start + size].reshape(4, -1, size)
        return piece.transpose(1, 0, 2).reshape(-1, 4 * size).astype(F32)

    mlp_own = owned(mlp_sum)
    attn_own = owned(jnp.concatenate([qk_sum, vo_sum], axis=1))
    gate_own, up_own, down_own = (whole(mlp_own, wide * i, units) for i in range(3))
    query_own, key_own, value_own, output_own = (whole(attn_own, part * i, part) for i in range(4))

    def gain_of(pairs):
        local = sum(jnp.sum(w.astype(F32) * g, axis=1) for w, g in pairs)
        return local + swap(local, "t")

    mlp_gain = gain_of([(gate_weight, gate_own), (up_weight, up_own)])
    attn_gain = gain_of(
        [(query_weight, query_own), (key_weight, key_own), (value_weight, value_own)]
    )
    return (
        layer_output,
        input_grad,
        attn_gain,
        query_own * gain_attn,
        key_own * gain_attn,
        value_own * gain_attn,
        output_own.T,
        mlp_gain,
        gate_own * gain_mlp,
        up_own * gain_mlp,
        down_own.T,
    )


def solution(mesh):
    devices = mesh.devices.reshape(4, 4, 2, 2, 2)
    fine = Mesh(devices, ("y", "x", "l", "c", "t"))
    rows = P(GROUP + ("t",), None)
    gain, into, out = P(GROUP), P(GROUP, "t"), P("t", GROUP)
    return jax.shard_map(
        shards,
        mesh=fine,
        in_specs=(rows, gain, into, into, into, out, gain, into, into, out, rows),
        out_specs=(rows, rows, gain, into, into, into, out, gain, into, into, out),
        check_vma=False,
    )
```

time: 3270 us -> 572 us (0.17)
  waiting for transfers between devices: 2620 us -> 228 us
  blocking collectives: 427 us -> 0 us
  starting transfers between devices: 1.69 us -> 99.9 us
  matrix products: 149 us -> 86.3 us
  local copies, waits for them, and re-layouts: 16.7 us -> 71.6 us
  other arithmetic: 23.1 us -> 58.2 us
    reduce_scatter x9 -> x1, waiting for transfers between devices: 1910 us -> 0.01 us  [shards(): lax.psum_scatter(mlp_partial.astype(BF), ('y', 'x'), scatter_dimension=0,...]
    all_gather x10 -> x1, waiting for transfers between devices: 671 us -> 0.01 us  [shards(): mlp_weight = lax.all_gather(mlp_block, ('y', 'x'), axis=0, tiled=True)]
    unnamed x2 -> x0, blocking collectives: 427 us -> none
    ppermute x0 -> x78, waiting for transfers between devices: none -> 228 us  [the longest x48 200 us: move(): lax.ppermute(values, axis, [(place[s], place[(s + distance) % 4]) for s i...]
    ppermute x0 -> x78, starting transfers between devices: none -> 99.9 us  [the longest x48 76.5 us: move(): lax.ppermute(values, axis, [(place[s], place[(s + distance) % 4]) for s i...]
    dot_general x26 -> x25, matrix products: 146 us -> 83.1 us  [the longest x5 27.4 us: plain(): return jnp.dot(left, right, preferred_element_type=F32)]
    psum x2 -> x0, waiting for transfers between devices: 38.5 us -> none  [the longest x1 38.5 us: shards(): lax.psum((times_t(grad_gate, full_gate) + times_t(grad_up, full_up)).asty...]
  transfers between devices with their start and end apart: 21 -> 80, of which waited for: 17 -> 39; matrix products, arithmetic and copies ran while one was open for 4% -> 33% of each run, Pallas kernels for 0% -> 0%
where the time goes in v1:
time: 572 us; the launch traced here: 562 us
  waiting for transfers between devices  228 us (40%)
  starting transfers between devices  99.9 us (17%)
  matrix products  86.3 us (15%)
  local copies, waits for them, and re-layouts  71.6 us (13%)
  other arithmetic  58.2 us (10%)
  between operations  17.5 us (3%)
    ppermute x48, waiting for transfers between devices, move(): lax.ppermute(values, axis, [(place[s], place[(s + distance) % 4]) for s i...  200 us
    ppermute x48, starting transfers between devices, move(): lax.ppermute(values, axis, [(place[s], place[(s + distance) % 4]) for s i...  76.5 us
    unnamed x154, local copies, waits for them, and re-layouts  34.5 us
    ppermute x30, waiting for transfers between devices, swap(): return lax.ppermute(values, axis, [(0, 1), (1, 0)])  28.4 us
    dot_general x5, matrix products, plain(): return jnp.dot(left, right, preferred_element_type=F32)  27.4 us
    dot_general x5, matrix products, left_t(): lax.dot_general(left, right, (((0,), (0,)), ((), ())), preferred_element_...  26.9 us
    ppermute x30, starting transfers between devices, swap(): return lax.ppermute(values, axis, [(0, 1), (1, 0)])  23.4 us
    dot_general x5, matrix products, times_t(): lax.dot_general(left, right, (((1,), (1,)), ((), ())), preferred_element_...  18.2 us
  transfers between devices with their start and end apart: 80, of which 39 were waited for; matrix products, arithmetic and copies ran while one was open for 33% of the time, Pallas kernels for 0%

profile of v1, /device:TPU:0, one launch (start us, length us, event | category | flops | bytes accessed | tf_op | source)
XLA Modules:
  0.0 561.8 jit_solution(11055073827946285017)
XLA Ops:
  10.6 4.0 collective-permute-start
  31.6 9.7 %collective-permute-done.8 = bf16[2,32,1024]{2,1,0:T(8,128)(2,1)S(1)} collective-permute-done((bf16[2,32,1024]{2,1,0:T(8,128)(2,1)S(1)}, bf16[2,32,1024]{2,1,0:T(8,128)(2,1)S(1)}, u32[]{:S(2)}, u32[]{:S(2)}) %collective-permute-start.8) | collective-permute-done | bytes 131104 | tf_op jit(solution)/shard_map/ppermute | solution.py:38
  42.4 6.8 %collective-permute-done.33 = bf16[2,32,2304]{2,1,0:T(8,128)(2,1)S(1)} collective-permute-done((bf16[2,32,2304]{2,1,0:T(8,128)(2,1)S(1)}, bf16[2,32,2304]{2,1,0:T(8,128)(2,1)S(1)}, u32[]{:S(2)}, u32[]{:S(2)}) %collective-permute-start.33) | collective-permute-done | bytes 294944 | tf_op jit(solution)/shard_map/ppermute | solution.py:38
  56.8 5.4 collective-permute-done.10
  62.2 3.1 collective-permute-start.11
  65.3 6.1 %collective-permute-done.11 = bf16[128,512]{1,0:T(8,128)(2,1)S(1)} collective-permute-done((bf16[128,512]{1,0:T(8,128)(2,1)S(1)}, bf16[128,512]{1,0:T(8,128)(2,1)S(1)}, u32[]{:S(2)}, u32[]{:S(2)}) %collective-permute-start.11) | collective-permute-done | bytes 131104 | tf_op jit(solution)/shard_map/ppermute | solution.py:34
  71.4 3.1 collective-permute-start.15
  79.1 6.1 %collective-permute-done.16 = bf16[128,512]{1,0:T(8,128)(2,1)S(1)} collective-permute-done((bf16[128,512]{1,0:T(8,128)(2,1)S(1)}, bf16[128,512]{1,0:T(8,128)(2,1)S(1)}, u32[]{:S(2)}, u32[]{:S(2)}) %collective-permute-start.16) | collective-permute-done | bytes 131104 | tf_op jit(solution)/shard_map/ppermute | solution.py:34
  86.4 8.9 %collective-permute-done.17 = bf16[128,512]{1,0:T(8,128)(2,1)S(1)} collective-permute-done((bf16[128,512]{1,0:T(8,128)(2,1)S(1)}, bf16[128,512]{1,0:T(8,128)(2,1)S(1)}, u32[]{:S(2)}, u32[]{:S(2)}) %collective-permute-start.17) | collective-permute-done | bytes 131104 | tf_op jit(solution)/shard_map/ppermute | solution.py:34
  104.5 16.8 %collective-permute-done.12 = bf16[4,128,512]{2,1,0:T(8,128)(2,1)S(1)} collective-permute-done((bf16[4,128,512]{2,1,0:T(8,128)(2,1)S(1)}, bf16[4,128,512]{2,1,0:T(8,128)(2,1)S(1)}, u32[]{:S(2)}, u32[]{:S(2)}) %collective-permute-start.12) | collective-permute-done | bytes 524320 | tf_op jit(solution)/shard_map/ppermute | solution.py:34
  123.3 3.0 collective-permute-done.13
  126.6 17.5 %collective-permute-done.14 = bf16[4,128,512]{2,1,0:T(8,128)(2,1)S(1)} collective-permute-done((bf16[4,128,512]{2,1,0:T(8,128)(2,1)S(1)}, bf16[4,128,512]{2,1,0:T(8,128)(2,1)S(1)}, u32[]{:S(2)}, u32[]{:S(2)}) %collective-permute-start.14) | collective-permute-done | bytes 524320 | tf_op jit(solution)/shard_map/ppermute | solution.py:34
  155.8 4.5 convolution_convert_fusion.8
  171.9 9.7 %collective-permute-start.41 = (bf16[128,2048]{1,0:T(8,128)(2,1)S(1)}, bf16[128,2048]{1,0:T(8,128)(2,1)S(1)}, u32[]{:S(2)}, u32[]{:S(2)}) collective-permute-start(bf16[128,2048]{1,0:T(8,128)(2,1)S(1)} %copy-done.15), channel_id=1, source_target_pairs={{0,2},{2,0},{1,3},{3,1},{4,6},{6,4},{5,7},{7,5},{8,10},{10,8},{9,1... | collective-permute-start | bytes 1572872 | tf_op jit(solution)/shard_map/ppermute | solution.py:38
  189.7 3.5 collective-permute-done.39
  193.2 4.1 collective-permute-start.24
  200.4 6.3 %collective-permute-done.22 = bf16[128,2048]{1,0:T(8,128)(2,1)S(1)} collective-permute-done((bf16[128,2048]{1,0:T(8,128)(2,1)S(1)}, bf16[128,2048]{1,0:T(8,128)(2,1)S(1)}, u32[]{:S(2)}, u32[]{:S(2)}) %collective-permute-start.22) | collective-permute-done | bytes 524320 | tf_op jit(solution)/shard_map/ppermute | solution.py:34
  206.7 10.1 %collective-permute-done.24 = bf16[128,2048]{1,0:T(8,128)(2,1)S(1)} collective-permute-done((bf16[128,2048]{1,0:T(8,128)(2,1)S(1)}, bf16[128,2048]{1,0:T(8,128)(2,1)S(1)}, u32[]{:S(2)}, u32[]{:S(2)}) %collective-permute-start.24) | collective-permute-done | bytes 524320 | tf_op jit(solution)/shard_map/ppermute | solution.py:34
  224.8 10.0 %collective-permute-done.25 = bf16[128,2048]{1,0:T(8,128)(2,1)S(1)} collective-permute-done((bf16[128,2048]{1,0:T(8,128)(2,1)S(1)}, bf16[128,2048]{1,0:T(8,128)(2,1)S(1)}, u32[]{:S(2)}, u32[]{:S(2)}) %collective-permute-start.25) | collective-permute-done | bytes 524320 | tf_op jit(solution)/shard_map/ppermute | solution.py:34
  235.6 6.6 %collective-permute-done.26 = bf16[128,2048]{1,0:T(8,128)(2,1)S(1)} collective-permute-done((bf16[128,2048]{1,0:T(8,128)(2,1)S(1)}, bf16[128,2048]{1,0:T(8,128)(2,1)S(1)}, u32[]{:S(2)}, u32[]{:S(2)}) %collective-permute-start.26) | collective-permute-done | bytes 524320 | tf_op jit(solution)/shard_map/ppermute | solution.py:34
  248.1 10.2 %fusion.4 = f32[1024,1536]{1,0:T(8,128)S(1)} fusion(bf16[1024,2048]{1,0:T(8,128)(2,1)} %constant_dynamic-update-slice_fusion.8, bf16[2048,2304]{1,0:T(8,128)(2,1)} %all-gather.2.cloned.1.call-done), kind=kOutput, calls=%fused_computation.7 | convolution fusion | flops 6442450944 | bytes 16777216 | tf_op jit(solution)/shard_map/dot_general | solution.py:21
  258.3 6.6 %multiply_convert_fusion.1 = (bf16[1024,768]{1,0:T(8,128)(2,1)S(1)}, bf16[1024,768]{1,0:T(8,128)(2,1)S(1)}, bf16[1024,768]{1,0:T(8,128)(2,1)S(1)}) fusion(f32[1024,1536]{1,0:T(8,128)S(1)} %fusion.4, bf16[1024,2048]{1,0:T(8,128)(2,1)} %constant_dynamic-update-slice_fusion.16, bf16[2048,2304]{1,0:T(8,128)(2,1)S(1)} %copy-done.61), kind=kOutput, calls=%fused_computation.19 | convolution fusion | flops 3232235520 | bytes 18350080 | tf_op jit(solution)/shard_map/dot_general | solution.py:21
  264.9 3.7 convolution_convert_fusion.2
  271.2 6.9 %fusion.6 = bf16[1024,2048]{1,0:T(8,128)(2,1)S(1)} fusion(bf16[2048,2304]{1,0:T(8,128)(2,1)S(1)} %copy-done.61, bf16[1024,768]{1,0:T(8,128)(2,1)S(1)} %get-tuple-element.21, bf16[1024,768]{1,0:T(8,128)(2,1)S(1)} %get-tuple-element.20), kind=kOutput, calls=%fused_computation.13 | convolution fusion | flops 6450839552 | bytes 13631488 | tf_op jit(solution)/shard_map/dot_general | solution.py:25
  278.1 11.2 %convolution_convert_fusion = bf16[2048,1536]{0,1:T(8,128)(2,1)S(1)} fusion(bf16[1024,2048]{1,0:T(8,128)(2,1)} %constant_dynamic-update-slice_fusion.8, bf16[1024,768]{1,0:T(8,128)(2,1)S(1)} %get-tuple-element.21, bf16[1024,768]{1,0:T(8,128)(2,1)S(1)} %get-tuple-element.20), kind=kOutput, calls=%fused_computation.4 | convolution fusion | flops 6451888128 | bytes 13631488 | tf_op jit(solution)/shard_map/dot_general | solution.py:29
  291.3 5.9 %convolution_convert_fusion.3 = bf16[2048,768]{0,1:T(8,128)(2,1)S(1)} fusion(bf16[1024,2048]{1,0:T(8,128)(2,1)} %constant_dynamic-update-slice_fusion.16, bf16[1024,768]{1,0:T(8,128)(2,1)S(1)} %get-tuple-element.26), kind=kOutput, calls=%fused_computation.16 | convolution fusion | flops 3222798336 | bytes 8912896 | tf_op jit(solution)/shard_map/dot_general | solution.py:29
  297.2 11.4 %pad_maximum_fusion = bf16[2048,2304]{0,1:T(8,128)(2,1)} fusion(bf16[2048,768]{0,1:T(8,128)(2,1)S(1)} %convolution_convert_fusion.3, bf16[2048,1536]{0,1:T(8,128)(2,1)S(1)} %convolution_convert_fusion), kind=kLoop, calls=%fused_computation.2 | loop fusion | flops 18874368 | bytes 18874368 | tf_op jit(solution)/shard_map/concatenate | solution.py:261
  308.6 12.6 %copy.298 = bf16[2048,2304]{1,0:T(8,128)(2,1)} copy(bf16[2048,2304]{0,1:T(8,128)(2,1)} %pad_maximum_fusion) | data formatting | bytes 18874368
  321.2 3.3 fusion.137
  332.9 3.2 collective-permute-start.47
  336.1 15.9 %collective-permute-done.35 = bf16[128,2048]{1,0:T(8,128)(2,1)S(1)} collective-permute-done((bf16[128,2048]{1,0:T(8,128)(2,1)S(1)}, bf16[128,2048]{1,0:T(8,128)(2,1)S(1)}, u32[]{:S(2)}, u32[]{:S(2)}) %collective-permute-start.35) | collective-permute-done | bytes 524320 | tf_op jit(solution)/shard_map/ppermute | solution.py:34
  352.1 10.2 %collective-permute-done.46 = bf16[128,2048]{1,0:T(8,128)(2,1)S(1)} collective-permute-done((bf16[128,2048]{1,0:T(8,128)(2,1)S(1)}, bf16[128,2048]{1,0:T(8,128)(2,1)S(1)}, u32[]{:S(2)}, u32[]{:S(2)}) %collective-permute-start.46) | collective-permute-done | bytes 524320 | tf_op jit(solution)/shard_map/ppermute | solution.py:34
  363.8 10.3 %collective-permute-done.48 = bf16[128,2048]{1,0:T(8,128)(2,1)S(1)} collective-permute-done((bf16[128,2048]{1,0:T(8,128)(2,1)S(1)}, bf16[128,2048]{1,0:T(8,128)(2,1)S(1)}, u32[]{:S(2)}, u32[]{:S(2)}) %collective-permute-start.48) | collective-permute-done | bytes 524320 | tf_op jit(solution)/shard_map/ppermute | solution.py:34
  381.4 6.4 %copy.295 = bf16[2048,1024]{1,0:T(8,128)(2,1)} copy(bf16[2048,1024]{0,1:T(8,128)(2,1)} %bitcast.440) | data formatting | bytes 8388608 | tf_op jit(solution)/shard_map/dot_general | solution.py:29
  387.8 6.3 %collective-permute-done.49 = bf16[128,2048]{1,0:T(8,128)(2,1)} collective-permute-done((bf16[128,2048]{1,0:T(8,128)(2,1)}, bf16[128,2048]{1,0:T(8,128)(2,1)}, u32[]{:S(2)}, u32[]{:S(2)}) %collective-permute-start.49) | collective-permute-done | bytes 524320 | tf_op jit(solution)/shard_map/ppermute | solution.py:34
  396.0 7.8 %collective-permute-done.50 = bf16[128,2048]{1,0:T(8,128)(2,1)S(1)} collective-permute-done((bf16[128,2048]{1,0:T(8,128)(2,1)}, bf16[128,2048]{1,0:T(8,128)(2,1)S(1)}, u32[]{:S(2)}, u32[]{:S(2)}) %collective-permute-start.50) | collective-permute-done | bytes 524320 | tf_op jit(solution)/shard_map/ppermute | solution.py:34
  409.4 3.8 convolution_convert_fusion.7
  426.2 4.9 convolution_convert_fusion.4
  433.7 3.2 collective-permute-start.61
  438.1 6.5 %copy.296 = bf16[2048,1024]{1,0:T(8,128)(2,1)} copy(bf16[2048,1024]{0,1:T(8,128)(2,1)} %bitcast.443) | data formatting | bytes 8388608 | tf_op jit(solution)/shard_map/dot_general | solution.py:29
  449.6 3.6 convolution_convert_fusion.5
  469.9 9.8 %collective-permute-done.66 = bf16[4,128,512]{2,1,0:T(8,128)(2,1)S(1)} collective-permute-done((bf16[4,128,512]{2,1,0:T(8,128)(2,1)S(1)}, bf16[4,128,512]{2,1,0:T(8,128)(2,1)S(1)}, u32[]{:S(2)}, u32[]{:S(2)}) %collective-permute-start.66) | collective-permute-done | bytes 524320 | tf_op jit(solution)/shard_map/ppermute | solution.py:34
  482.5 3.0 collective-permute-start.70
  497.1 4.2 collective-permute-done.73
  508.1 3.0 convert_add_fusion
  518.0 9.8 %collective-permute-done.57 = bf16[128,2048]{1,0:T(8,128)(2,1)S(1)} collective-permute-done((bf16[128,2048]{1,0:T(8,128)(2,1)}, bf16[128,2048]{1,0:T(8,128)(2,1)S(1)}, u32[]{:S(2)}, u32[]{:S(2)}) %collective-permute-start.57) | collective-permute-done | bytes 524320 | tf_op jit(solution)/shard_map/ppermute | solution.py:34
  527.8 8.5 %collective-permute-done.58 = bf16[128,2048]{1,0:T(8,128)(2,1)S(1)} collective-permute-done((bf16[128,2048]{1,0:T(8,128)(2,1)}, bf16[128,2048]{1,0:T(8,128)(2,1)S(1)}, u32[]{:S(2)}, u32[]{:S(2)}) %collective-permute-start.58) | collective-permute-done | bytes 524320 | tf_op jit(solution)/shard_map/ppermute | solution.py:34
  540.9 2.8 fusion.29
  (446 shorter events, 203.9 us)
Async XLA Ops:
  7.2 240.9 %all-gather.2.cloned.1.call-start = ((), (), s32[]{:S(2)}) async-start(), calls=%async_computation.1 | async-start | bytes 10027008 | tf_op jit(solution)/shard_map/all_gather | solution.py:217
  10.6 88.3 %collective-permute-start = (bf16[128,2048]{1,0:T(8,128)(2,1)S(1)}, bf16[128,2048]{1,0:T(8,128)(2,1)S(1)}, u32[]{:S(2)}, u32[]{:S(2)}) collective-permute-start(bf16[128,2048]{1,0:T(8,128)(2,1)S(1)} %get-tuple-element.19), channel_id=1, source_target_pairs={{0,1},{4,5},{1,0},{5,4},{2,3},{6,7},{3,2},{7,6},{8,9},{12,13},{9,8... | collective-permute-start | bytes 1572872 | tf_op jit(solution)/shard_map/ppermute | solution.py:34
  14.6 85.1 %collective-permute-start.1 = (bf16[128,2048]{1,0:T(8,128)(2,1)S(1)}, bf16[128,2048]{1,0:T(8,128)(2,1)S(1)}, u32[]{:S(2)}, u32[]{:S(2)}) collective-permute-start(bf16[128,2048]{1,0:T(8,128)(2,1)S(1)} %get-tuple-element.19), channel_id=1, source_target_pairs={{0,5},{4,0},{1,4},{5,1},{2,7},{6,2},{3,6},{7,3},{8,13},{12,8},{9,1... | collective-permute-start | bytes 1572872 | tf_op jit(solution)/shard_map/ppermute | solution.py:34
  15.3 85.9 %collective-permute-start.2 = (bf16[128,2048]{1,0:T(8,128)(2,1)S(1)}, bf16[128,2048]{1,0:T(8,128)(2,1)S(1)}, u32[]{:S(2)}, u32[]{:S(2)}) collective-permute-start(bf16[128,2048]{1,0:T(8,128)(2,1)S(1)} %get-tuple-element.19), channel_id=1, source_target_pairs={{0,4},{4,1},{1,5},{5,0},{2,6},{6,3},{3,7},{7,2},{8,12},{12,9},{9,1... | collective-permute-start | bytes 1572872 | tf_op jit(solution)/shard_map/ppermute | solution.py:34
  16.6 86.4 %collective-permute-start.3 = (bf16[128,2048]{1,0:T(8,128)(2,1)S(1)}, bf16[128,2048]{1,0:T(8,128)(2,1)}, u32[]{:S(2)}, u32[]{:S(2)}) collective-permute-start(bf16[128,2048]{1,0:T(8,128)(2,1)S(1)} %get-tuple-element.19), channel_id=1, source_target_pairs={{0,2},{2,0},{1,3},{3,1},{4,6},{6,4},{5,7},{7,5},{8,10},{10,8},{9,1... | collective-permute-start | bytes 1572872 | tf_op jit(solution)/shard_map/ppermute | solution.py:38
  50.2 466.5 %reduce-scatter.4.cloned.1.call-start = ((), (), s32[]{:S(2)}) async-start(), calls=%async_computation.2 | async-start | bytes 10027008 | tf_op jit(solution)/shard_map/reduce_scatter | solution.py:262
  95.3 26.0 %collective-permute-start.12 = (bf16[4,128,512]{2,1,0:T(8,128)(2,1)S(1)}, bf16[4,128,512]{2,1,0:T(8,128)(2,1)S(1)}, u32[]{:S(2)}, u32[]{:S(2)}) collective-permute-start(bf16[4,128,512]{2,1,0:T(8,128)(2,1)S(1)} %bitcast_dynamic-update-slice_fusion.12), channel_id=1, source_target_pairs={{0,96},{32,0},{64,32},{96,64},{1,97},{33,1},{65,33},{97,65},{2,98}... | collective-permute-start | bytes 1572872 | tf_op jit(solution)/shard_map/ppermute | solution.py:34
  98.9 27.4 %collective-permute-start.13 = (bf16[4,128,512]{2,1,0:T(8,128)(2,1)S(1)}, bf16[4,128,512]{2,1,0:T(8,128)(2,1)S(1)}, u32[]{:S(2)}, u32[]{:S(2)}) collective-permute-start(bf16[4,128,512]{2,1,0:T(8,128)(2,1)S(1)} %bitcast_dynamic-update-slice_fusion.12), channel_id=1, source_target_pairs={{0,32},{32,64},{64,96},{96,0},{1,33},{33,65},{65,97},{97,1},{2,34}... | collective-permute-start | bytes 1572872 | tf_op jit(solution)/shard_map/ppermute | solution.py:34
  99.7 44.3 %collective-permute-start.14 = (bf16[4,128,512]{2,1,0:T(8,128)(2,1)S(1)}, bf16[4,128,512]{2,1,0:T(8,128)(2,1)S(1)}, u32[]{:S(2)}, u32[]{:S(2)}) collective-permute-start(bf16[4,128,512]{2,1,0:T(8,128)(2,1)S(1)} %bitcast_dynamic-update-slice_fusion.12), channel_id=1, source_target_pairs={{0,64},{32,96},{64,0},{96,32},{1,65},{33,97},{65,1},{97,33},{2,66}... | collective-permute-start | bytes 1572872 | tf_op jit(solution)/shard_map/ppermute | solution.py:34
  101.2 42.9 %collective-permute-start.18 = (bf16[4,128,512]{2,1,0:T(8,128)(2,1)S(1)}, bf16[4,128,512]{2,1,0:T(8,128)(2,1)S(1)}, u32[]{:S(2)}, u32[]{:S(2)}) collective-permute-start(bf16[4,128,512]{2,1,0:T(8,128)(2,1)S(1)} %bitcast_dynamic-update-slice_fusion.8), channel_id=1, source_target_pairs={{0,24},{8,0},{16,8},{24,16},{1,25},{9,1},{17,9},{25,17},{2,26},{10... | collective-permute-start | bytes 1572872 | tf_op jit(solution)/shard_map/ppermute | solution.py:34
  103.0 42.6 %collective-permute-start.19 = (bf16[4,128,512]{2,1,0:T(8,128)(2,1)S(1)}, bf16[4,128,512]{2,1,0:T(8,128)(2,1)S(1)}, u32[]{:S(2)}, u32[]{:S(2)}) collective-permute-start(bf16[4,128,512]{2,1,0:T(8,128)(2,1)S(1)} %bitcast_dynamic-update-slice_fusion.8), channel_id=1, source_target_pairs={{0,8},{8,16},{16,24},{24,0},{1,9},{9,17},{17,25},{25,1},{2,10},{10... | collective-permute-start | bytes 1572872 | tf_op jit(solution)/shard_map/ppermute | solution.py:34
  121.3 25.9 %collective-permute-start.20 = (bf16[4,128,512]{2,1,0:T(8,128)(2,1)S(1)}, bf16[4,128,512]{2,1,0:T(8,128)(2,1)S(1)}, u32[]{:S(2)}, u32[]{:S(2)}) collective-permute-start(bf16[4,128,512]{2,1,0:T(8,128)(2,1)S(1)} %bitcast_dynamic-update-slice_fusion.8), channel_id=1, source_target_pairs={{0,16},{8,24},{16,0},{24,8},{1,17},{9,25},{17,1},{25,9},{2,18},{10... | collective-permute-start | bytes 1572872 | tf_op jit(solution)/shard_map/ppermute | solution.py:34
  126.3 21.8 %collective-permute-start.4 = (bf16[128,2048]{1,0:T(8,128)(2,1)S(1)}, bf16[128,2048]{1,0:T(8,128)(2,1)S(1)}, u32[]{:S(2)}, u32[]{:S(2)}) collective-permute-start(bf16[128,2048]{1,0:T(8,128)(2,1)S(1)} %collective-permute-done), channel_id=1, source_target_pairs={{0,2},{2,0},{1,3},{3,1},{4,6},{6,4},{5,7},{7,5},{8,10},{10,8},{9,1... | collective-permute-start | bytes 1572872 | tf_op jit(solution)/shard_map/ppermute | solution.py:38
  167.2 18.0 %collective-permute-start.21 = (bf16[512,2048]{1,0:T(8,128)(2,1)S(1)}, bf16[512,2048]{1,0:T(8,128)(2,1)S(1)}, u32[]{:S(2)}, u32[]{:S(2)}) collective-permute-start(bf16[512,2048]{1,0:T(8,128)(2,1)S(1)} %slice.410), channel_id=1, source_target_pairs={{0,2},{2,0},{1,3},{3,1},{4,6},{6,4},{5,7},{7,5},{8,10},{10,8},{9,1... | collective-permute-start | bytes 6291464 | tf_op jit(solution)/shard_map/ppermute | solution.py:38
  169.3 24.0 %collective-permute-start.39 = (bf16[128,2048]{1,0:T(8,128)(2,1)S(1)}, bf16[128,2048]{1,0:T(8,128)(2,1)S(1)}, u32[]{:S(2)}, u32[]{:S(2)}) collective-permute-start(bf16[128,2048]{1,0:T(8,128)(2,1)S(1)} %copy-done.15), channel_id=1, source_target_pairs={{0,5},{4,0},{1,4},{5,1},{2,7},{6,2},{3,6},{7,3},{8,13},{12,8},{9,1... | collective-permute-start | bytes 1572872 | tf_op jit(solution)/shard_map/ppermute | solution.py:34
  171.9 26.3 %collective-permute-start.40 = (bf16[128,2048]{1,0:T(8,128)(2,1)S(1)}, bf16[128,2048]{1,0:T(8,128)(2,1)S(1)}, u32[]{:S(2)}, u32[]{:S(2)}) collective-permute-start(bf16[128,2048]{1,0:T(8,128)(2,1)S(1)} %copy-done.15), channel_id=1, source_target_pairs={{0,4},{4,1},{1,5},{5,0},{2,6},{6,3},{3,7},{7,2},{8,12},{12,9},{9,1... | collective-permute-start | bytes 1572872 | tf_op jit(solution)/shard_map/ppermute | solution.py:34
  171.9 27.2 %collective-permute-start.41 = (bf16[128,2048]{1,0:T(8,128)(2,1)S(1)}, bf16[128,2048]{1,0:T(8,128)(2,1)S(1)}, u32[]{:S(2)}, u32[]{:S(2)}) collective-permute-start(bf16[128,2048]{1,0:T(8,128)(2,1)S(1)} %copy-done.15), channel_id=1, source_target_pairs={{0,2},{2,0},{1,3},{3,1},{4,6},{6,4},{5,7},{7,5},{8,10},{10,8},{9,1... | collective-permute-start | bytes 1572872 | tf_op jit(solution)/shard_map/ppermute | solution.py:38
  186.4 20.3 %collective-permute-start.22 = (bf16[128,2048]{1,0:T(8,128)(2,1)S(1)}, bf16[128,2048]{1,0:T(8,128)(2,1)S(1)}, u32[]{:S(2)}, u32[]{:S(2)}) collective-permute-start(bf16[128,2048]{1,0:T(8,128)(2,1)S(1)} %get-tuple-element.46), channel_id=1, source_target_pairs={{0,4},{4,1},{1,5},{5,0},{2,6},{6,3},{3,7},{7,2},{8,12},{12,9},{9,1... | collective-permute-start | bytes 1572872 | tf_op jit(solution)/shard_map/ppermute | solution.py:34
  187.7 19.1 %collective-permute-start.23 = (bf16[128,2048]{1,0:T(8,128)(2,1)S(1)}, bf16[128,2048]{1,0:T(8,128)(2,1)S(1)}, u32[]{:S(2)}, u32[]{:S(2)}) collective-permute-start(bf16[128,2048]{1,0:T(8,128)(2,1)S(1)} %get-tuple-element.48), channel_id=1, source_target_pairs={{0,5},{4,0},{1,4},{5,1},{2,7},{6,2},{3,6},{7,3},{8,13},{12,8},{9,1... | collective-permute-start | bytes 1572872 | tf_op jit(solution)/shard_map/ppermute | solution.py:34
  193.2 23.6 %collective-permute-start.24 = (bf16[128,2048]{1,0:T(8,128)(2,1)S(1)}, bf16[128,2048]{1,0:T(8,128)(2,1)S(1)}, u32[]{:S(2)}, u32[]{:S(2)}) collective-permute-start(bf16[128,2048]{1,0:T(8,128)(2,1)S(1)} %get-tuple-element.47), channel_id=1, source_target_pairs={{0,1},{4,5},{1,0},{5,4},{2,3},{6,7},{3,2},{7,6},{8,9},{12,13},{9,8... | collective-permute-start | bytes 1572872 | tf_op jit(solution)/shard_map/ppermute | solution.py:34
  198.2 21.4 %collective-permute-start.42 = (bf16[128,2048]{1,0:T(8,128)(2,1)S(1)}, bf16[128,2048]{1,0:T(8,128)(2,1)S(1)}, u32[]{:S(2)}, u32[]{:S(2)}) collective-permute-start(bf16[128,2048]{1,0:T(8,128)(2,1)S(1)} %collective-permute-done.38), channel_id=1, source_target_pairs={{0,2},{2,0},{1,3},{3,1},{4,6},{6,4},{5,7},{7,5},{8,10},{10,8},{9,1... | collective-permute-start | bytes 1572872 | tf_op jit(solution)/shard_map/ppermute | solution.py:38
  199.0 24.0 %collective-permute-start.43 = (bf16[128,2048]{1,0:T(8,128)(2,1)S(1)}, bf16[128,2048]{1,0:T(8,128)(2,1)S(1)}, u32[]{:S(2)}, u32[]{:S(2)}) collective-permute-start(bf16[128,2048]{1,0:T(8,128)(2,1)S(1)} %collective-permute-done.39), channel_id=1, source_target_pairs={{0,2},{2,0},{1,3},{3,1},{4,6},{6,4},{5,7},{7,5},{8,10},{10,8},{9,1... | collective-permute-start | bytes 1572872 | tf_op jit(solution)/shard_map/ppermute | solution.py:38
  206.7 17.2 %collective-permute-start.44 = (bf16[128,2048]{1,0:T(8,128)(2,1)S(1)}, bf16[128,2048]{1,0:T(8,128)(2,1)S(1)}, u32[]{:S(2)}, u32[]{:S(2)}) collective-permute-start(bf16[128,2048]{1,0:T(8,128)(2,1)S(1)} %collective-permute-done.40), channel_id=1, source_target_pairs={{0,2},{2,0},{1,3},{3,1},{4,6},{6,4},{5,7},{7,5},{8,10},{10,8},{9,1... | collective-permute-start | bytes 1572872 | tf_op jit(solution)/shard_map/ppermute | solution.py:38
  220.5 21.7 %collective-permute-start.26 = (bf16[128,2048]{1,0:T(8,128)(2,1)S(1)}, bf16[128,2048]{1,0:T(8,128)(2,1)S(1)}, u32[]{:S(2)}, u32[]{:S(2)}) collective-permute-start(bf16[128,2048]{1,0:T(8,128)(2,1)S(1)} %get-tuple-element.15), channel_id=1, source_target_pairs={{0,5},{4,0},{1,4},{5,1},{2,7},{6,2},{3,6},{7,3},{8,13},{12,8},{9,1... | collective-permute-start | bytes 1572872 | tf_op jit(solution)/shard_map/ppermute | solution.py:34
  223.9 19.9 %collective-permute-start.27 = (bf16[128,2048]{1,0:T(8,128)(2,1)S(1)}, bf16[128,2048]{1,0:T(8,128)(2,1)S(1)}, u32[]{:S(2)}, u32[]{:S(2)}) collective-permute-start(bf16[128,2048]{1,0:T(8,128)(2,1)S(1)} %get-tuple-element.15), channel_id=1, source_target_pairs={{0,4},{4,1},{1,5},{5,0},{2,6},{6,3},{3,7},{7,2},{8,12},{12,9},{9,1... | collective-permute-start | bytes 1572872 | tf_op jit(solution)/shard_map/ppermute | solution.py:34
  224.8 19.9 %collective-permute-start.28 = (bf16[128,2048]{1,0:T(8,128)(2,1)S(1)}, bf16[128,2048]{1,0:T(8,128)(2,1)S(1)}, u32[]{:S(2)}, u32[]{:S(2)}) collective-permute-start(bf16[128,2048]{1,0:T(8,128)(2,1)S(1)} %get-tuple-element.15), channel_id=1, source_target_pairs={{0,2},{2,0},{1,3},{3,1},{4,6},{6,4},{5,7},{7,5},{8,10},{10,8},{9,1... | collective-permute-start | bytes 1572872 | tf_op jit(solution)/shard_map/ppermute | solution.py:38
  270.2 51.0 %collective-permute-start.34 = (bf16[512,2048]{1,0:T(8,128)(2,1)}, bf16[512,2048]{1,0:T(8,128)(2,1)}, u32[]{:S(2)}, u32[]{:S(2)}) collective-permute-start(bf16[512,2048]{1,0:T(8,128)(2,1)} %slice.424), channel_id=1, source_target_pairs={{0,2},{2,0},{1,3},{3,1},{4,6},{6,4},{5,7},{7,5},{8,10},{10,8},{9,1... | collective-permute-start | bytes 6291464 | tf_op jit(solution)/shard_map/ppermute | solution.py:38
  290.8 38.8 %collective-permute-start.45 = (bf16[512,2048]{1,0:T(8,128)(2,1)}, bf16[512,2048]{1,0:T(8,128)(2,1)}, u32[]{:S(2)}, u32[]{:S(2)}) collective-permute-start(bf16[512,2048]{1,0:T(8,128)(2,1)} %slice.430), channel_id=1, source_target_pairs={{0,2},{2,0},{1,3},{3,1},{4,6},{6,4},{5,7},{7,5},{8,10},{10,8},{9,1... | collective-permute-start | bytes 6291464 | tf_op jit(solution)/shard_map/ppermute | solution.py:38
  324.7 27.2 %collective-permute-start.35 = (bf16[128,2048]{1,0:T(8,128)(2,1)S(1)}, bf16[128,2048]{1,0:T(8,128)(2,1)S(1)}, u32[]{:S(2)}, u32[]{:S(2)}) collective-permute-start(bf16[128,2048]{1,0:T(8,128)(2,1)S(1)} %get-tuple-element.43), channel_id=1, source_target_pairs={{0,4},{4,1},{1,5},{5,0},{2,6},{6,3},{3,7},{7,2},{8,12},{12,9},{9,1... | collective-permute-start | bytes 1572872 | tf_op jit(solution)/shard_map/ppermute | solution.py:34
  326.5 25.4 %collective-permute-start.36 = (bf16[128,2048]{1,0:T(8,128)(2,1)S(1)}, bf16[128,2048]{1,0:T(8,128)(2,1)S(1)}, u32[]{:S(2)}, u32[]{:S(2)}) collective-permute-start(bf16[128,2048]{1,0:T(8,128)(2,1)S(1)} %get-tuple-element.45), channel_id=1, source_target_pairs={{0,5},{4,0},{1,4},{5,1},{2,7},{6,2},{3,6},{7,3},{8,13},{12,8},{9,1... | collective-permute-start | bytes 1572872 | tf_op jit(solution)/shard_map/ppermute | solution.py:34
  328.0 24.0 %collective-permute-start.37 = (bf16[128,2048]{1,0:T(8,128)(2,1)S(1)}, bf16[128,2048]{1,0:T(8,128)(2,1)S(1)}, u32[]{:S(2)}, u32[]{:S(2)}) collective-permute-start(bf16[128,2048]{1,0:T(8,128)(2,1)S(1)} %get-tuple-element.44), channel_id=1, source_target_pairs={{0,1},{4,5},{1,0},{5,4},{2,3},{6,7},{3,2},{7,6},{8,9},{12,13},{9,8... | collective-permute-start | bytes 1572872 | tf_op jit(solution)/shard_map/ppermute | solution.py:34
  332.4 29.9 %collective-permute-start.46 = (bf16[128,2048]{1,0:T(8,128)(2,1)S(1)}, bf16[128,2048]{1,0:T(8,128)(2,1)S(1)}, u32[]{:S(2)}, u32[]{:S(2)}) collective-permute-start(bf16[128,2048]{1,0:T(8,128)(2,1)S(1)} %get-tuple-element.40), channel_id=1, source_target_pairs={{0,4},{4,1},{1,5},{5,0},{2,6},{6,3},{3,7},{7,2},{8,12},{12,9},{9,1... | collective-permute-start | bytes 1572872 | tf_op jit(solution)/shard_map/ppermute | solution.py:34
  332.9 30.9 %collective-permute-start.47 = (bf16[128,2048]{1,0:T(8,128)(2,1)S(1)}, bf16[128,2048]{1,0:T(8,128)(2,1)S(1)}, u32[]{:S(2)}, u32[]{:S(2)}) collective-permute-start(bf16[128,2048]{1,0:T(8,128)(2,1)S(1)} %get-tuple-element.42), channel_id=1, source_target_pairs={{0,5},{4,0},{1,4},{5,1},{2,7},{6,2},{3,6},{7,3},{8,13},{12,8},{9,1... | collective-permute-start | bytes 1572872 | tf_op jit(solution)/shard_map/ppermute | solution.py:34
  352.0 22.2 %collective-permute-start.48 = (bf16[128,2048]{1,0:T(8,128)(2,1)S(1)}, bf16[128,2048]{1,0:T(8,128)(2,1)S(1)}, u32[]{:S(2)}, u32[]{:S(2)}) collective-permute-start(bf16[128,2048]{1,0:T(8,128)(2,1)S(1)} %get-tuple-element.41), channel_id=1, source_target_pairs={{0,1},{4,5},{1,0},{5,4},{2,3},{6,7},{3,2},{7,6},{8,9},{12,13},{9,8... | collective-permute-start | bytes 1572872 | tf_op jit(solution)/shard_map/ppermute | solution.py:34
  379.3 24.4 %collective-permute-start.50 = (bf16[128,2048]{1,0:T(8,128)(2,1)}, bf16[128,2048]{1,0:T(8,128)(2,1)S(1)}, u32[]{:S(2)}, u32[]{:S(2)}) collective-permute-start(bf16[128,2048]{1,0:T(8,128)(2,1)} %get-tuple-element.12), channel_id=1, source_target_pairs={{0,5},{4,0},{1,4},{5,1},{2,7},{6,2},{3,6},{7,3},{8,13},{12,8},{9,1... | collective-permute-start | bytes 1572872 | tf_op jit(solution)/shard_map/ppermute | solution.py:34
  381.2 23.4 %collective-permute-start.51 = (bf16[128,2048]{1,0:T(8,128)(2,1)}, bf16[128,2048]{1,0:T(8,128)(2,1)S(1)}, u32[]{:S(2)}, u32[]{:S(2)}) collective-permute-start(bf16[128,2048]{1,0:T(8,128)(2,1)} %get-tuple-element.12), channel_id=1, source_target_pairs={{0,4},{4,1},{1,5},{5,0},{2,6},{6,3},{3,7},{7,2},{8,12},{12,9},{9,1... | collective-permute-start | bytes 1572872 | tf_op jit(solution)/shard_map/ppermute | solution.py:34
  387.8 18.3 %collective-permute-start.52 = (bf16[128,2048]{1,0:T(8,128)(2,1)}, bf16[128,2048]{1,0:T(8,128)(2,1)S(1)}, u32[]{:S(2)}, u32[]{:S(2)}) collective-permute-start(bf16[128,2048]{1,0:T(8,128)(2,1)} %get-tuple-element.12), channel_id=1, source_target_pairs={{0,2},{2,0},{1,3},{3,1},{4,6},{6,4},{5,7},{7,5},{8,10},{10,8},{9,1... | collective-permute-start | bytes 1572872 | tf_op jit(solution)/shard_map/ppermute | solution.py:38
  433.7 26.6 %collective-permute-start.60 = (bf16[4,128,512]{2,1,0:T(8,128)(2,1)}, bf16[4,128,512]{2,1,0:T(8,128)(2,1)}, u32[]{:S(2)}, u32[]{:S(2)}) collective-permute-start(bf16[4,128,512]{2,1,0:T(8,128)(2,1)} %get-tuple-element.31), channel_id=1, source_target_pairs={{0,8},{8,16},{16,24},{24,0},{1,9},{9,17},{17,25},{25,1},{2,10},{10... | collective-permute-start | bytes 1572872 | tf_op jit(solution)/shard_map/ppermute | solution.py:34
  433.7 31.1 %collective-permute-start.61 = (bf16[4,128,512]{2,1,0:T(8,128)(2,1)}, bf16[4,128,512]{2,1,0:T(8,128)(2,1)}, u32[]{:S(2)}, u32[]{:S(2)}) collective-permute-start(bf16[4,128,512]{2,1,0:T(8,128)(2,1)} %get-tuple-element.33), channel_id=1, source_target_pairs={{0,24},{8,0},{16,8},{24,16},{1,25},{9,1},{17,9},{25,17},{2,26},{10... | collective-permute-start | bytes 1572872 | tf_op jit(solution)/shard_map/ppermute | solution.py:34
  436.9 27.9 %collective-permute-start.62 = (bf16[4,128,512]{2,1,0:T(8,128)(2,1)}, bf16[4,128,512]{2,1,0:T(8,128)(2,1)}, u32[]{:S(2)}, u32[]{:S(2)}) collective-permute-start(bf16[4,128,512]{2,1,0:T(8,128)(2,1)} %get-tuple-element.32), channel_id=1, source_target_pairs={{0,16},{8,24},{16,0},{24,8},{1,17},{9,25},{17,1},{25,9},{2,18},{10... | collective-permute-start | bytes 1572872 | tf_op jit(solution)/shard_map/ppermute | solution.py:34
  454.6 25.2 %collective-permute-start.66 = (bf16[4,128,512]{2,1,0:T(8,128)(2,1)S(1)}, bf16[4,128,512]{2,1,0:T(8,128)(2,1)S(1)}, u32[]{:S(2)}, u32[]{:S(2)}) collective-permute-start(bf16[4,128,512]{2,1,0:T(8,128)(2,1)S(1)} %get-tuple-element.34), channel_id=1, source_target_pairs={{0,32},{32,64},{64,96},{96,0},{1,33},{33,65},{65,97},{97,1},{2,34}... | collective-permute-start | bytes 1572872 | tf_op jit(solution)/shard_map/ppermute | solution.py:34
  456.4 23.4 %collective-permute-start.67 = (bf16[4,128,512]{2,1,0:T(8,128)(2,1)S(1)}, bf16[4,128,512]{2,1,0:T(8,128)(2,1)S(1)}, u32[]{:S(2)}, u32[]{:S(2)}) collective-permute-start(bf16[4,128,512]{2,1,0:T(8,128)(2,1)S(1)} %get-tuple-element.35), channel_id=1, source_target_pairs={{0,96},{32,0},{64,32},{96,64},{1,97},{33,1},{65,33},{97,65},{2,98}... | collective-permute-start | bytes 1572872 | tf_op jit(solution)/shard_map/ppermute | solution.py:34
  460.3 21.6 %collective-permute-start.68 = (bf16[4,128,512]{2,1,0:T(8,128)(2,1)S(1)}, bf16[4,128,512]{2,1,0:T(8,128)(2,1)S(1)}, u32[]{:S(2)}, u32[]{:S(2)}) collective-permute-start(bf16[4,128,512]{2,1,0:T(8,128)(2,1)S(1)} %get-tuple-element.36), channel_id=1, source_target_pairs={{0,64},{32,96},{64,0},{96,32},{1,65},{33,97},{65,1},{97,33},{2,66}... | collective-permute-start | bytes 1572872 | tf_op jit(solution)/shard_map/ppermute | solution.py:34
  466.6 18.8 %collective-permute-start.63 = (bf16[128,512]{1,0:T(8,128)(2,1)S(1)}, bf16[128,512]{1,0:T(8,128)(2,1)S(1)}, u32[]{:S(2)}, u32[]{:S(2)}) collective-permute-start(bf16[128,512]{1,0:T(8,128)(2,1)S(1)} %get-tuple-element.66), channel_id=1, source_target_pairs={{0,32},{32,64},{64,96},{96,0},{1,33},{33,65},{65,97},{97,1},{2,34}... | collective-permute-start | bytes 393224 | tf_op jit(solution)/shard_map/ppermute | solution.py:34
  467.2 19.9 %collective-permute-start.64 = (bf16[128,512]{1,0:T(8,128)(2,1)S(1)}, bf16[128,512]{1,0:T(8,128)(2,1)S(1)}, u32[]{:S(2)}, u32[]{:S(2)}) collective-permute-start(bf16[128,512]{1,0:T(8,128)(2,1)S(1)} %get-tuple-element.68), channel_id=1, source_target_pairs={{0,96},{32,0},{64,32},{96,64},{1,97},{33,1},{65,33},{97,65},{2,98}... | collective-permute-start | bytes 393224 | tf_op jit(solution)/shard_map/ppermute | solution.py:34
  513.6 22.7 %collective-permute-start.58 = (bf16[128,2048]{1,0:T(8,128)(2,1)}, bf16[128,2048]{1,0:T(8,128)(2,1)S(1)}, u32[]{:S(2)}, u32[]{:S(2)}) collective-permute-start(bf16[128,2048]{1,0:T(8,128)(2,1)} %get-tuple-element.39), channel_id=1, source_target_pairs={{0,5},{4,0},{1,4},{5,1},{2,7},{6,2},{3,6},{7,3},{8,13},{12,8},{9,1... | collective-permute-start | bytes 1572872 | tf_op jit(solution)/shard_map/ppermute | solution.py:34
  515.6 22.1 %collective-permute-start.59 = (bf16[128,2048]{1,0:T(8,128)(2,1)}, bf16[128,2048]{1,0:T(8,128)(2,1)S(1)}, u32[]{:S(2)}, u32[]{:S(2)}) collective-permute-start(bf16[128,2048]{1,0:T(8,128)(2,1)} %get-tuple-element.38), channel_id=1, source_target_pairs={{0,1},{4,5},{1,0},{5,4},{2,3},{6,7},{3,2},{7,6},{8,9},{12,13},{9,8... | collective-permute-start | bytes 1572872 | tf_op jit(solution)/shard_map/ppermute | solution.py:34
  517.9 21.7 %collective-permute-start.75 = (bf16[2,32,2304]{2,1,0:T(8,128)(2,1)S(1)}, bf16[2,32,2304]{2,1,0:T(8,128)(2,1)S(1)}, u32[]{:S(2)}, u32[]{:S(2)}) collective-permute-start(bf16[2,32,2304]{2,1,0:T(8,128)(2,1)S(1)} %select_bitcast_fusion.1), channel_id=1, source_target_pairs={{0,2},{2,0},{1,3},{3,1},{4,6},{6,4},{5,7},{7,5},{8,10},{10,8},{9,1... | collective-permute-start | bytes 884744 | tf_op jit(solution)/shard_map/ppermute | solution.py:38
  (96 other events, 1047.7 us)
Sparse Core Ops, SparseCore 0:
  50.3 100.2 all-gather.1
  321.3 86.5 reduce-scatter.3
